TPU v7x, 32 devices: a whole 2x2x4 slice. The times are simulated.
32 devices in a mesh: fsdp: 4 (over x, core), chan: 8 (over z, y).
Axes of the slice: x: 2, y: 2, z: 4, core: 2. Of those that a mesh axis runs over, the one named last changes fastest.
Arguments:
- hidden: bfloat16 [512, 4096], P('fsdp'), may hold values from -6 to 6
- conv_out: bfloat16 [512, 8192], P('fsdp', 'chan'), may hold values from -6 to 6
- state_in: float32 [8192, 16], P('chan'), may hold values from -6 to 6
- gate_weight: bfloat16 [4096, 8192], P('fsdp', 'chan'), may hold values from -0.09375 to 0.09375
- xproj_weight: bfloat16 [8192, 288], P('chan'), may hold values from -0.0625 to 0.0625
- dt_weight: bfloat16 [256, 8192], P(None, 'chan'), may hold values from -0.375 to 0.375
- dt_bias: float32 [8192], P('chan'), may hold values from -7 to -1
- a_log: float32 [8192, 16], P('chan'), may hold values from -1.5 to 2.77
- skip_gain: float32 [8192], P('chan'), may hold values from 0.25 to 1
- out_weight: bfloat16 [4096, 8192], P('fsdp', 'chan'), may hold values from -0.0625 to 0.0625
Outputs:
- mixed: bfloat16 [512, 4096], P(('fsdp', 'chan'))
All inputs are finite; a program needn't handle non-finite values.
Results may differ from a plain program's by a relative error of at most 0.007.
Values may be sent and summed in bfloat16 or wider, within the bound.
A program may use at most 64 MiB of HBM per device.

v0:
```python
import jax
import jax.numpy as jnp
from jax import lax
from jax.sharding import PartitionSpec as P

STATE = 16
RANK = 256
BLOCK = 16


def shards(
    hidden,
    conv_out,
    state_in,
    gate_weight,
    xproj_weight,
    dt_weight,
    dt_bias,
    a_log,
    skip_gain,
    out_weight,
):
    rows_here, channels = conv_out.shape
    partial_value = jnp.dot(conv_out, xproj_weight, preferred_element_type=jnp.float32)
    projected = lax.psum(partial_value, "chan")
    step_low = projected[:, :RANK].astype(jnp.bfloat16)
    in_coef = projected[:, RANK : RANK + STATE]
    out_coef = projected[:, RANK + STATE :]
    step_size = jax.nn.softplus(
        jnp.dot(step_low, dt_weight, preferred_element_type=jnp.float32) + dt_bias
    )
    decay_rate = -jnp.exp(a_log)
    inputs = conv_out.astype(jnp.float32)
    blocks = rows_here // BLOCK
    position_rows = lax.broadcasted_iota(jnp.int32, (BLOCK, BLOCK), 0)
    position_cols = lax.broadcasted_iota(jnp.int32, (BLOCK, BLOCK), 1)
    causal_mask = position_rows >= position_cols

    def block_step(carry_state, block_items):
        step_blk, input_blk, in_blk, out_blk = block_items
        within = jnp.cumsum(step_blk, axis=0)
        spread = jnp.where(causal_mask[:, :, None], within[:, None, :] - within[None, :, :], 0.0)
        weights = jnp.where(
            causal_mask[:, :, None, None], jnp.exp(spread[:, :, :, None] * decay_rate), 0.0
        )
        driven = (step_blk * input_blk)[:, :, None] * in_blk[:, None, :]
        states = jnp.einsum("tscn,scn->tcn", weights, driven, precision=lax.Precision.HIGHEST)
        states = states + jnp.exp(within[:, :, None] * decay_rate) * carry_state[None]
        block_out = jnp.einsum("tcn,tn->tc", states, out_blk, precision=lax.Precision.HIGHEST)
        return (states[-1], block_out)

    def split_blocks(values):
        return values.reshape((blocks, BLOCK) + values.shape[1:])

    empty_state = jnp.zeros((channels, STATE), jnp.float32)
    last_state, local_out = lax.scan(
        block_step,
        empty_state,
        (
            split_blocks(step_size),
            split_blocks(inputs),
            split_blocks(in_coef),
            split_blocks(out_coef),
        ),
    )
    local_out = local_out.reshape((rows_here, channels))
    total_step = jnp.sum(step_size, axis=0)
    totals, finals = (
        lax.all_gather(total_step[None], "fsdp", axis=0, tiled=True),
        lax.all_gather(last_state[None], "fsdp", axis=0, tiled=True),
    )
    position = lax.axis_index("fsdp")
    sources = jnp.arange(totals.shape[0], dtype=jnp.int32)
    earlier_mask = sources < position
    through_sum = jnp.cumsum(totals, axis=0)
    before_sum = jnp.sum(jnp.where(earlier_mask[:, None], totals, 0.0), axis=0)
    gap_steps = jnp.where(earlier_mask[:, None], before_sum[None, :] - through_sum, 0.0)
    factor = jnp.where(
        earlier_mask[:, None, None], jnp.exp(gap_steps[:, :, None] * decay_rate), 0.0
    )
    entering = (
        jnp.sum(factor * finals, axis=0) + jnp.exp(before_sum[:, None] * decay_rate) * state_in
    )
    through = jnp.cumsum(step_size, axis=0)
    carried = jnp.einsum(
        "tcn,tn->tc",
        jnp.exp(through[:, :, None] * decay_rate) * entering[None],
        out_coef,
        precision=lax.Precision.HIGHEST,
    )
    scanned = local_out + carried
    gate_full, out_full = (
        lax.all_gather(gate_weight, "fsdp", axis=0, tiled=True),
        lax.all_gather(out_weight, "fsdp", axis=0, tiled=True),
    )
    gate_pre = jnp.dot(hidden, gate_full, preferred_element_type=jnp.float32)
    gated_out = ((scanned + skip_gain * inputs) * jax.nn.silu(gate_pre)).astype(jnp.bfloat16)
    summed = lax.psum_scatter(
        lax.dot_general(
            gated_out, out_full, (((1,), (1,)), ((), ())), preferred_element_type=jnp.float32
        ),
        "chan",
        scatter_dimension=0,
        tiled=True,
    )
    mixed = summed.astype(jnp.bfloat16)
    return mixed


def solution(mesh):
    placed = (
        P("fsdp", None),
        P("fsdp", "chan"),
        P("chan", None),
        P("fsdp", "chan"),
        P("chan", None),
        P(None, "chan"),
        P("chan"),
        P("chan", None),
        P("chan"),
        P("fsdp", "chan"),
    )
    return jax.shard_map(
        shards, mesh=mesh, in_specs=placed, out_specs=P(("fsdp", "chan"), None), check_vma=False
    )
```

profile of v0, /device:TPU:0, one launch (start us, length us, event | category | flops | bytes accessed | tf_op | source)
XLA Modules:
  0.0 405.1 jit_solution(6566140458010184439)
XLA Ops:
  13.8 70.3 %all-reduce.2.cloned.1.call-done = f32[128,288]{0,1:T(8,128)} async-done(((f32[128,288]{0,1:T(8,128)}), f32[128,288]{0,1:T(8,128)}) %all-reduce.2.cloned.1.call-update) | async-done | bytes 147472 | tf_op jit(solution)/shard_map/psum | solution.py:25
  87.6 197.4 %while.14 = (s32[]{:T(128)}, f32[1024,16]{1,0:T(8,128)}, f32[8,16,1024]{2,1,0:T(8,128)}, f32[8,16,1024]{2,1,0:T(8,128)S(1)}, f32[8,16,1024]{2,1,0:T(8,128)S(1)},...) while((s32[]{:T(128)}, f32[1024,16]{1,0:T(8,128)}, ...), condition=%wide.region_3.4_spmd.clone.clone, body=%wide.region_1.3_spmd.clone.clone.sunk | while | flops 21496064 | bytes 20454916 | solution.py:56
  98.0 5.3 %bitcast_add_fusion.3 = f32[16,1024,16]{2,1,0:T(8,128)S(1)} fusion(f32[1024,16,16]{1,0,2:T(8,128)} %copy.72, f32[1024,16]{1,0:T(8,128)S(1)} %copy-done.1, f32[1024,16]{1,0:T(8,128)S(1)} %copy.73, f32[16,1024]{1,0:T(8,128)S(1)} %reduce_window_sum.38), kind=kLoop, calls=%fused_computation.2.clone.1 | loop fusion | flops 786432 | bytes 2293760 | tf_op jit(solution)/shard_map/while/body/eval_jaxpr/add | solution.py:48
  103.3 7.4 %fusion.31 = f32[16,1,1024]{2,1,0:T(1,128)S(1)} fusion(f32[16,1024,16]{2,1,0:T(8,128)S(1)} %bitcast_add_fusion.3, f32[16,16,1]{1,2,0:T(1,128)S(1)} %bitcast.79), kind=kOutput, calls=%fused_computation.34.clone.1 | convolution fusion | flops 3145728 | bytes 1115136 | tf_op jit(solution)/shard_map/while/body/eval_jaxpr/tcn,tn->tc/dot_general | solution.py:49
  122.7 5.4 %bitcast_add_fusion.3 = f32[16,1024,16]{2,1,0:T(8,128)S(1)} fusion(f32[1024,16,16]{1,0,2:T(8,128)} %copy.72, f32[1024,16]{1,0:T(8,128)S(1)} %copy-done.1, f32[1024,16]{1,0:T(8,128)S(1)} %copy.73, f32[16,1024]{1,0:T(8,128)S(1)} %reduce_window_sum.38), kind=kLoop, calls=%fused_computation.2.clone.1 | loop fusion | flops 786432 | bytes 2293760 | tf_op jit(solution)/shard_map/while/body/eval_jaxpr/add | solution.py:48
  128.1 7.4 %fusion.31 = f32[16,1,1024]{2,1,0:T(1,128)S(1)} fusion(f32[16,1024,16]{2,1,0:T(8,128)S(1)} %bitcast_add_fusion.3, f32[16,16,1]{1,2,0:T(1,128)S(1)} %bitcast.79), kind=kOutput, calls=%fused_computation.34.clone.1 | convolution fusion | flops 3145728 | bytes 1115136 | tf_op jit(solution)/shard_map/while/body/eval_jaxpr/tcn,tn->tc/dot_general | solution.py:49
  147.4 5.3 %bitcast_add_fusion.3 = f32[16,1024,16]{2,1,0:T(8,128)S(1)} fusion(f32[1024,16,16]{1,0,2:T(8,128)} %copy.72, f32[1024,16]{1,0:T(8,128)S(1)} %copy-done.1, f32[1024,16]{1,0:T(8,128)S(1)} %copy.73, f32[16,1024]{1,0:T(8,128)S(1)} %reduce_window_sum.38), kind=kLoop, calls=%fused_computation.2.clone.1 | loop fusion | flops 786432 | bytes 2293760 | tf_op jit(solution)/shard_map/while/body/eval_jaxpr/add | solution.py:48
  152.8 7.4 %fusion.31 = f32[16,1,1024]{2,1,0:T(1,128)S(1)} fusion(f32[16,1024,16]{2,1,0:T(8,128)S(1)} %bitcast_add_fusion.3, f32[16,16,1]{1,2,0:T(1,128)S(1)} %bitcast.79), kind=kOutput, calls=%fused_computation.34.clone.1 | convolution fusion | flops 3145728 | bytes 1115136 | tf_op jit(solution)/shard_map/while/body/eval_jaxpr/tcn,tn->tc/dot_general | solution.py:49
  172.1 5.3 %bitcast_add_fusion.3 = f32[16,1024,16]{2,1,0:T(8,128)S(1)} fusion(f32[1024,16,16]{1,0,2:T(8,128)} %copy.72, f32[1024,16]{1,0:T(8,128)S(1)} %copy-done.1, f32[1024,16]{1,0:T(8,128)S(1)} %copy.73, f32[16,1024]{1,0:T(8,128)S(1)} %reduce_window_sum.38), kind=kLoop, calls=%fused_computation.2.clone.1 | loop fusion | flops 786432 | bytes 2293760 | tf_op jit(solution)/shard_map/while/body/eval_jaxpr/add | solution.py:48
  177.4 7.4 %fusion.31 = f32[16,1,1024]{2,1,0:T(1,128)S(1)} fusion(f32[16,1024,16]{2,1,0:T(8,128)S(1)} %bitcast_add_fusion.3, f32[16,16,1]{1,2,0:T(1,128)S(1)} %bitcast.79), kind=kOutput, calls=%fused_computation.34.clone.1 | convolution fusion | flops 3145728 | bytes 1115136 | tf_op jit(solution)/shard_map/while/body/eval_jaxpr/tcn,tn->tc/dot_general | solution.py:49
  196.8 5.3 %bitcast_add_fusion.3 = f32[16,1024,16]{2,1,0:T(8,128)S(1)} fusion(f32[1024,16,16]{1,0,2:T(8,128)} %copy.72, f32[1024,16]{1,0:T(8,128)S(1)} %copy-done.1, f32[1024,16]{1,0:T(8,128)S(1)} %copy.73, f32[16,1024]{1,0:T(8,128)S(1)} %reduce_window_sum.38), kind=kLoop, calls=%fused_computation.2.clone.1 | loop fusion | flops 786432 | bytes 2293760 | tf_op jit(solution)/shard_map/while/body/eval_jaxpr/add | solution.py:48
  202.1 7.4 %fusion.31 = f32[16,1,1024]{2,1,0:T(1,128)S(1)} fusion(f32[16,1024,16]{2,1,0:T(8,128)S(1)} %bitcast_add_fusion.3, f32[16,16,1]{1,2,0:T(1,128)S(1)} %bitcast.79), kind=kOutput, calls=%fused_computation.34.clone.1 | convolution fusion | flops 3145728 | bytes 1115136 | tf_op jit(solution)/shard_map/while/body/eval_jaxpr/tcn,tn->tc/dot_general | solution.py:49
  221.4 5.3 %bitcast_add_fusion.3 = f32[16,1024,16]{2,1,0:T(8,128)S(1)} fusion(f32[1024,16,16]{1,0,2:T(8,128)} %copy.72, f32[1024,16]{1,0:T(8,128)S(1)} %copy-done.1, f32[1024,16]{1,0:T(8,128)S(1)} %copy.73, f32[16,1024]{1,0:T(8,128)S(1)} %reduce_window_sum.38), kind=kLoop, calls=%fused_computation.2.clone.1 | loop fusion | flops 786432 | bytes 2293760 | tf_op jit(solution)/shard_map/while/body/eval_jaxpr/add | solution.py:48
  226.8 7.4 %fusion.31 = f32[16,1,1024]{2,1,0:T(1,128)S(1)} fusion(f32[16,1024,16]{2,1,0:T(8,128)S(1)} %bitcast_add_fusion.3, f32[16,16,1]{1,2,0:T(1,128)S(1)} %bitcast.79), kind=kOutput, calls=%fused_computation.34.clone.1 | convolution fusion | flops 3145728 | bytes 1115136 | tf_op jit(solution)/shard_map/while/body/eval_jaxpr/tcn,tn->tc/dot_general | solution.py:49
  246.1 5.3 %bitcast_add_fusion.3 = f32[16,1024,16]{2,1,0:T(8,128)S(1)} fusion(f32[1024,16,16]{1,0,2:T(8,128)} %copy.72, f32[1024,16]{1,0:T(8,128)S(1)} %copy-done.1, f32[1024,16]{1,0:T(8,128)S(1)} %copy.73, f32[16,1024]{1,0:T(8,128)S(1)} %reduce_window_sum.38), kind=kLoop, calls=%fused_computation.2.clone.1 | loop fusion | flops 786432 | bytes 2293760 | tf_op jit(solution)/shard_map/while/body/eval_jaxpr/add | solution.py:48
  251.4 7.4 %fusion.31 = f32[16,1,1024]{2,1,0:T(1,128)S(1)} fusion(f32[16,1024,16]{2,1,0:T(8,128)S(1)} %bitcast_add_fusion.3, f32[16,16,1]{1,2,0:T(1,128)S(1)} %bitcast.79), kind=kOutput, calls=%fused_computation.34.clone.1 | convolution fusion | flops 3145728 | bytes 1115136 | tf_op jit(solution)/shard_map/while/body/eval_jaxpr/tcn,tn->tc/dot_general | solution.py:49
  270.8 5.3 %bitcast_add_fusion.3 = f32[16,1024,16]{2,1,0:T(8,128)S(1)} fusion(f32[1024,16,16]{1,0,2:T(8,128)} %copy.72, f32[1024,16]{1,0:T(8,128)S(1)} %copy-done.1, f32[1024,16]{1,0:T(8,128)S(1)} %copy.73, f32[16,1024]{1,0:T(8,128)S(1)} %reduce_window_sum.38), kind=kLoop, calls=%fused_computation.2.clone.1 | loop fusion | flops 786432 | bytes 2293760 | tf_op jit(solution)/shard_map/while/body/eval_jaxpr/add | solution.py:48
  276.1 7.4 %fusion.31 = f32[16,1,1024]{2,1,0:T(1,128)S(1)} fusion(f32[16,1024,16]{2,1,0:T(8,128)S(1)} %bitcast_add_fusion.3, f32[16,16,1]{1,2,0:T(1,128)S(1)} %bitcast.79), kind=kOutput, calls=%fused_computation.34.clone.1 | convolution fusion | flops 3145728 | bytes 1115136 | tf_op jit(solution)/shard_map/while/body/eval_jaxpr/tcn,tn->tc/dot_general | solution.py:49
  285.5 5.3 %all-gather = f32[4096]{0:T(1024)S(1)} all-gather(f32[1024]{0:T(1024)S(1)} %get-tuple-element.165), channel_id=2, replica_groups=mesh['fsdp'=4,'chan'=8] {'fsdp'}, dimensions={0}, use_global_device_ids=true | all-gather | bytes 20480 | tf_op jit(solution)/shard_map/all_gather | solution.py:69
  290.9 16.2 %all-gather.1 = f32[4096,16]{1,0:T(8,128)S(1)} all-gather(f32[1024,16]{1,0:T(8,128)} %get-tuple-element.57), channel_id=3, replica_groups=mesh['fsdp'=4,'chan'=8] {'fsdp'}, dimensions={0}, use_global_device_ids=true | all-gather | bytes 327680 | tf_op jit(solution)/shard_map/all_gather | solution.py:70
  309.3 6.5 %fusion.2 = f32[128,1,1024]{2,1,0:T(1,128)} fusion(f32[128,16,1]{1,2,0:T(1,128)S(1)} %copy.61, f32[1024,16]{0,1:T(8,128)S(1)} %multiply_add_fusion, f32[1024,16]{0,1:T(8,128)S(1)} %get-tuple-element.253, f32[128,1024]{1,0:T(8,128)S(1)} %reduce_window_sum.33), kind=kOutput, calls=%fused_computation.12 | convolution fusion | flops 29360128 | bytes 1187840 | tf_op jit(solution)/shard_map/tcn,tn->tc/dot_general | solution.py:85
  315.8 4.8 %fusion.11 = bf16[128,1024]{1,0:T(8,128)(2,1)S(1)} fusion(f32[8,16,1024]{2,1,0:T(8,128)S(1)} %copy-done.9, f32[128,1,1024]{2,1,0:T(1,128)} %fusion.2, f32[1024]{0:T(1024)S(1)} %copy-done.10, bf16[128,1024]{1,0:T(8,128)(2,1)S(1)} %copy-done.6, bf16[128,4096]{1,0:T(8,128)(2,1)S(1)} %copy-done, bf16[4096,1024]{1,0:T(8,128)(2,1)} %all-gather.5.cloned.1.call-done), kind=kOutput, calls=%fused_computation.25 | convolution fusion | flops 1075052544 | bytes 11014144 | tf_op jit(solution)/shard_map/dot_general | solution.py:96
  320.7 7.6 %fusion.15 = f32[128,4096]{1,0:T(8,128)} fusion(bf16[128,1024]{1,0:T(8,128)(2,1)S(1)} %fusion.11, bf16[4096,1024]{1,0:T(8,128)(2,1)} %all-gather.7.cloned.1.call-done), kind=kOutput, calls=%fused_computation.36 | convolution fusion | flops 1073741824 | bytes 10747904 | tf_op jit(solution)/shard_map/dot_general | solution.py:99
  328.3 67.7 %reduce-scatter.2.cloned.1.call-done = f32[16,4096]{1,0:T(8,128)} async-done(((f32[128,4096]{1,0:T(8,128)}), f32[16,4096]{1,0:T(8,128)}) %reduce-scatter.2.cloned.1.call-update) | async-done | bytes 262160 | tf_op jit(solution)/shard_map/reduce_scatter | solution.py:98
  (227 shorter events, 109.3 us)
Async XLA Ops:
  7.4 308.4 %copy-start = (bf16[128,4096]{1,0:T(8,128)(2,1)S(1)}, bf16[128,4096]{1,0:T(8,128)(2,1)}, u32[]{:S(2)}) copy-start(bf16[128,4096]{1,0:T(8,128)(2,1)} %param.12) | copy-start | bytes 3145732
  7.4 76.8 %all-reduce.2.cloned.1.call-start = ((), (), s32[]{:S(2)}) async-start(), calls=%async_computation.1 | async-start | bytes 294912 | tf_op jit(solution)/shard_map/psum | solution.py:25
  9.6 306.1 %all-gather.5.cloned.1.call-start = ((), (), s32[]{:S(2)}) async-start(), calls=%async_computation.2 | async-start | bytes 10485760 | tf_op jit(solution)/shard_map/all_gather | solution.py:93
  10.2 310.5 %all-gather.7.cloned.1.call-start = ((), (), s32[]{:S(2)}) async-start(), calls=%async_computation.3 | async-start | bytes 10485760 | tf_op jit(solution)/shard_map/all_gather | solution.py:94
  10.8 385.3 %reduce-scatter.2.cloned.1.call-start = ((), (), s32[]{:S(2)}) async-start(), calls=%async_computation.4 | async-start | bytes 2359296 | tf_op jit(solution)/shard_map/reduce_scatter | solution.py:98
  87.6 221.6 %copy-start.7 = (f32[1024,16]{0,1:T(8,128)S(1)}, f32[1024,16]{0,1:T(8,128)}, u32[]{:S(2)}) copy-start(f32[1024,16]{0,1:T(8,128)} %param.19) | copy-start | bytes 196612
  87.6 221.6 %copy-start.8 = (f32[1024,16]{0,1:T(8,128)S(1)}, f32[1024,16]{0,1:T(8,128)}, u32[]{:S(2)}) copy-start(f32[1024,16]{0,1:T(8,128)} %param.14) | copy-start | bytes 196612
  103.3 8.9 %copy-start.3 = (f32[8,16,1024]{2,1,0:T(8,128)S(1)}, f32[8,16,1024]{2,1,0:T(8,128)}, u32[]{:S(2)}) copy-start(f32[8,16,1024]{2,1,0:T(8,128)} %copy-done.2) | copy-start | bytes 1572868 | tf_op jit(solution)/shard_map/while
  128.1 8.9 %copy-start.3 = (f32[8,16,1024]{2,1,0:T(8,128)S(1)}, f32[8,16,1024]{2,1,0:T(8,128)}, u32[]{:S(2)}) copy-start(f32[8,16,1024]{2,1,0:T(8,128)} %copy-done.2) | copy-start | bytes 1572868 | tf_op jit(solution)/shard_map/while
  128.1 8.9 %copy-start.5 = (f32[8,16,1024]{2,1,0:T(8,128)S(1)}, f32[8,16,1024]{2,1,0:T(8,128)}, u32[]{:S(2)}) copy-start(f32[8,16,1024]{2,1,0:T(8,128)} %copy-done.4) | copy-start | bytes 1572868 | tf_op jit(solution)/shard_map/while
  152.7 8.9 %copy-start.3 = (f32[8,16,1024]{2,1,0:T(8,128)S(1)}, f32[8,16,1024]{2,1,0:T(8,128)}, u32[]{:S(2)}) copy-start(f32[8,16,1024]{2,1,0:T(8,128)} %copy-done.2) | copy-start | bytes 1572868 | tf_op jit(solution)/shard_map/while
  152.7 8.9 %copy-start.5 = (f32[8,16,1024]{2,1,0:T(8,128)S(1)}, f32[8,16,1024]{2,1,0:T(8,128)}, u32[]{:S(2)}) copy-start(f32[8,16,1024]{2,1,0:T(8,128)} %copy-done.4) | copy-start | bytes 1572868 | tf_op jit(solution)/shard_map/while
  177.4 8.9 %copy-start.3 = (f32[8,16,1024]{2,1,0:T(8,128)S(1)}, f32[8,16,1024]{2,1,0:T(8,128)}, u32[]{:S(2)}) copy-start(f32[8,16,1024]{2,1,0:T(8,128)} %copy-done.2) | copy-start | bytes 1572868 | tf_op jit(solution)/shard_map/while
  177.4 8.9 %copy-start.5 = (f32[8,16,1024]{2,1,0:T(8,128)S(1)}, f32[8,16,1024]{2,1,0:T(8,128)}, u32[]{:S(2)}) copy-start(f32[8,16,1024]{2,1,0:T(8,128)} %copy-done.4) | copy-start | bytes 1572868 | tf_op jit(solution)/shard_map/while
  202.1 8.9 %copy-start.3 = (f32[8,16,1024]{2,1,0:T(8,128)S(1)}, f32[8,16,1024]{2,1,0:T(8,128)}, u32[]{:S(2)}) copy-start(f32[8,16,1024]{2,1,0:T(8,128)} %copy-done.2) | copy-start | bytes 1572868 | tf_op jit(solution)/shard_map/while
  202.1 8.9 %copy-start.5 = (f32[8,16,1024]{2,1,0:T(8,128)S(1)}, f32[8,16,1024]{2,1,0:T(8,128)}, u32[]{:S(2)}) copy-start(f32[8,16,1024]{2,1,0:T(8,128)} %copy-done.4) | copy-start | bytes 1572868 | tf_op jit(solution)/shard_map/while
  226.7 8.9 %copy-start.3 = (f32[8,16,1024]{2,1,0:T(8,128)S(1)}, f32[8,16,1024]{2,1,0:T(8,128)}, u32[]{:S(2)}) copy-start(f32[8,16,1024]{2,1,0:T(8,128)} %copy-done.2) | copy-start | bytes 1572868 | tf_op jit(solution)/shard_map/while
  251.4 8.9 %copy-start.3 = (f32[8,16,1024]{2,1,0:T(8,128)S(1)}, f32[8,16,1024]{2,1,0:T(8,128)}, u32[]{:S(2)}) copy-start(f32[8,16,1024]{2,1,0:T(8,128)} %copy-done.2) | copy-start | bytes 1572868 | tf_op jit(solution)/shard_map/while
  251.4 8.9 %copy-start.5 = (f32[8,16,1024]{2,1,0:T(8,128)S(1)}, f32[8,16,1024]{2,1,0:T(8,128)}, u32[]{:S(2)}) copy-start(f32[8,16,1024]{2,1,0:T(8,128)} %copy-done.4) | copy-start | bytes 1572868 | tf_op jit(solution)/shard_map/while
  276.1 8.9 %copy-start.3 = (f32[8,16,1024]{2,1,0:T(8,128)S(1)}, f32[8,16,1024]{2,1,0:T(8,128)}, u32[]{:S(2)}) copy-start(f32[8,16,1024]{2,1,0:T(8,128)} %copy-done.2) | copy-start | bytes 1572868 | tf_op jit(solution)/shard_map/while
  276.1 8.9 %copy-start.5 = (f32[8,16,1024]{2,1,0:T(8,128)S(1)}, f32[8,16,1024]{2,1,0:T(8,128)}, u32[]{:S(2)}) copy-start(f32[8,16,1024]{2,1,0:T(8,128)} %copy-done.4) | copy-start | bytes 1572868 | tf_op jit(solution)/shard_map/while
  285.0 30.8 %copy-start.6 = (bf16[128,1024]{1,0:T(8,128)(2,1)S(1)}, bf16[128,1024]{1,0:T(8,128)(2,1)}, u32[]{:S(2)}) copy-start(bf16[128,1024]{1,0:T(8,128)(2,1)} %param.13) | copy-start | bytes 786436
  285.0 30.8 %copy-start.10 = (f32[1024]{0:T(1024)S(1)}, f32[1024]{0:T(1024)}, u32[]{:S(2)}) copy-start(f32[1024]{0:T(1024)} %param.20) | copy-start | bytes 12292
  285.5 30.3 %copy-start.9 = (f32[8,16,1024]{2,1,0:T(8,128)S(1)}, f32[8,16,1024]{2,1,0:T(8,128)}, u32[]{:S(2)}) copy-start(f32[8,16,1024]{2,1,0:T(8,128)} %get-tuple-element.56) | copy-start | bytes 1572868
  (26 other events, 74.0 us)
Sparse Core Ops, SparseCore 0:
  11.5 72.5 all-reduce.1
  328.4 67.5 reduce-scatter.1
Sparse Core Ops, SparseCore 1:
  11.7 60.8 all-gather.4
  74.1 58.1 all-gather.6
where the time goes:
time: 406 us; the launch traced here: 405 us
  waiting for transfers between devices  139 us (34%)
  other arithmetic  85.7 us (21%)
  matrix products  81.9 us (20%)
  local copies, waits for them, and re-layouts  60.8 us (15%)
  blocking collectives  21.5 us (5%)
  between operations  15 us (4%)
    psum x1, waiting for transfers between devices, shards(): projected = lax.psum(partial_value, 'chan')  70.3 us
    reduce_scatter x1, waiting for transfers between devices, shards(): lax.psum_scatter(lax.dot_general(gated_out, out_full, (((1,), (1,)), ((),...  67.7 us
    dot_general x8, matrix products, block_step(): jnp.einsum('tcn,tn->tc', states, out_blk, precision=lax.Precision.HIGHEST)  59.1 us
    add x8, other arithmetic, block_step(): states + jnp.exp(within[:, :, None] * decay_rate) * carry_state[None]  42.3 us
    dot_general x8, local copies, waits for them, and re-layouts, block_step(): jnp.einsum('tscn,scn->tcn', weights, driven, precision=lax.Precision.HIGH...  36.9 us
    while x16, other arithmetic  35.3 us
    all_gather x1, blocking collectives, shards(): lax.all_gather(last_state[None], 'fsdp', axis=0, tiled=True)  16.2 us
    while x88, local copies, waits for them, and re-layouts  8.38 us
  transfers between devices with their start and end apart: 4, of which 2 were waited for; matrix products, arithmetic and copies ran while one was open for 52% of the time, Pallas kernels for 0%

commit v1 on v0

--- a/solution.py
+++ b/solution.py
@@ -1,6 +1,10 @@
+import functools
+
 import jax
 import jax.numpy as jnp
 from jax import lax
+from jax.experimental import pallas as pl
+from jax.experimental.pallas import tpu as pltpu
 from jax.sharding import PartitionSpec as P
 
 STATE = 16
@@ -8,7 +12,12 @@
 BLOCK = 16
 
 
-def shards(
+def running_sum(values):
+    lower = jnp.tril(jnp.ones((values.shape[0],) * 2, jnp.float32))
+    return jnp.dot(lower, values, precision=lax.Precision.HIGHEST)
+
+
+def generic_shards(
     hidden,
     conv_out,
     state_in,
@@ -38,7 +47,7 @@
 
     def block_step(carry_state, block_items):
         step_blk, input_blk, in_blk, out_blk = block_items
-        within = jnp.cumsum(step_blk, axis=0)
+        within = running_sum(step_blk)
         spread = jnp.where(causal_mask[:, :, None], within[:, None, :] - within[None, :, :], 0.0)
         weights = jnp.where(
             causal_mask[:, :, None, None], jnp.exp(spread[:, :, :, None] * decay_rate), 0.0
@@ -72,7 +81,7 @@
     position = lax.axis_index("fsdp")
     sources = jnp.arange(totals.shape[0], dtype=jnp.int32)
     earlier_mask = sources < position
-    through_sum = jnp.cumsum(totals, axis=0)
+    through_sum = running_sum(totals)
     before_sum = jnp.sum(jnp.where(earlier_mask[:, None], totals, 0.0), axis=0)
     gap_steps = jnp.where(earlier_mask[:, None], before_sum[None, :] - through_sum, 0.0)
     factor = jnp.where(
@@ -81,7 +90,7 @@
     entering = (
         jnp.sum(factor * finals, axis=0) + jnp.exp(before_sum[:, None] * decay_rate) * state_in
     )
-    through = jnp.cumsum(step_size, axis=0)
+    through = running_sum(step_size)
     carried = jnp.einsum(
         "tcn,tn->tc",
         jnp.exp(through[:, :, None] * decay_rate) * entering[None],
@@ -105,6 +114,349 @@
     )
     mixed = summed.astype(jnp.bfloat16)
     return mixed
+
+
+LANES = 128
+STEPS = 16
+
+
+def fused_kernel(
+    F,
+    G,
+    hidden,
+    conv,
+    state,
+    gate_w,
+    xproj,
+    dt_w,
+    dt_bias,
+    a_log,
+    skip,
+    out_w,
+    out,
+    pp,
+    pp_in,
+    conv_in,
+    hid_in,
+    pg,
+    gate_send,
+    gate_own,
+    gate_in,
+    steps_s,
+    drive_s,
+    tiled_s,
+    y_s,
+    gated,
+    po,
+    fin_in,
+    pp_ss,
+    pp_rs,
+    cv_ss,
+    cv_rs,
+    hd_ss,
+    hd_rs,
+    pg_ss,
+    pg_rs,
+    gt_ss,
+    gt_rs,
+    gd_ss,
+    gd_rs,
+    fo_ss,
+    fo_rs,
+):
+    f32, bf16 = jnp.float32, jnp.bfloat16
+    N = F * G
+    f, c = lax.axis_index("fsdp"), lax.axis_index("chan")
+    me = f * G + c
+    rows, channels = conv.shape
+    R, CS, DB = rows // G, channels // F, gate_w.shape[0]
+    wide = pp.shape[1]
+
+    def remote(src, dst, ss, rs, f2, c2):
+        return pltpu.make_async_remote_copy(
+            src_ref=src,
+            dst_ref=dst,
+            send_sem=ss,
+            recv_sem=rs,
+            device_id={"fsdp": f2, "chan": c2},
+            device_id_type=pl.DeviceIdType.MESH,
+        )
+
+    def at(base, size, step):
+        return pl.ds(pl.multiple_of(base * step, step), size)
+
+    barrier = pltpu.get_barrier_semaphore()
+
+    @pl.loop(1, N)
+    def _(p):
+        lin = lax.rem(me + p, N)
+        pl.semaphore_signal(
+            barrier,
+            inc=1,
+            device_id={"fsdp": lin // G, "chan": lax.rem(lin, G)},
+            device_id_type=pl.DeviceIdType.MESH,
+        )
+
+    pp[:, RANK:] = jnp.zeros((rows, wide - RANK), f32)
+    pp[:, : xproj.shape[1]] = jnp.dot(conv[...], xproj[...], preferred_element_type=f32)
+    pl.semaphore_wait(barrier, N - 1)
+
+    def pp_copy(j):
+        c2 = lax.rem(c + j, G)
+        return remote(pp.at[at(c2, R, R)], pp_in.at[c], pp_ss.at[c2], pp_rs.at[c], f, c2)
+
+    def conv_copy(f2):
+        return remote(conv.at[:, at(f2, CS, CS)], conv_in.at[f], cv_ss.at[f2], cv_rs.at[f], f2, c)
+
+    def hid_copy(f2):
+        return remote(hidden.at[:, at(f2, DB, DB)], hid_in.at[f], hd_ss.at[f2], hd_rs.at[f], f2, c)
+
+    pl.loop(1, G)(lambda j: pp_copy(j).start())
+    for j in range(1, F):
+        hid_copy(lax.rem(f + j, F)).start()
+        conv_copy(lax.rem(f + j, F)).start()
+    conv_in[f] = conv[:, at(f, CS, CS)]
+    hid_in[f] = hidden[:, at(f, DB, DB)]
+
+    def gate_copy(k, f2):
+        piece = at(k, rows, rows)
+        return remote(
+            gate_send.at[f2, piece], gate_in.at[f, piece], gt_ss.at[k * F + f2], gt_rs.at[k * F + f], f2, c
+        )
+
+    def gate_block(k):
+        piece = at(k, rows, rows)
+        lhs = hid_in[k]
+        for j in range(F):
+            f2 = lax.rem(f + j, F)
+            part = jnp.dot(lhs, gate_w[:, at(f2, CS, CS)], preferred_element_type=f32)
+            if j == 0:
+                gate_own[piece] = part
+            else:
+                gate_send[f2, piece] = part.astype(bf16)
+                gate_copy(k, f2).start()
+
+    gate_block(f)
+
+    total = pp[at(c, R, R)]
+    for j in range(1, G):
+        c2 = lax.rem(c + j, G)
+        remote(pp.at[at(c, R, R)], pp_in.at[c2], pp_ss.at[c2], pp_rs.at[c2], f, c2).wait_recv()
+        total = total + pp_in[c2]
+    high = total.astype(bf16)
+    low = (total[:, RANK:] - high[:, RANK:].astype(f32)).astype(bf16)
+    pg[at(me, R, R), :wide] = high
+    pg[at(me, R, R), wide:] = low
+
+    def pg_copy(f2, c2):
+        mine = pg.at[at(me, R, R)]
+        lin = f2 * G + c2
+        return remote(mine, mine, pg_ss.at[lin], pg_rs.at[me], f2, c2)
+
+    @pl.loop(1, N)
+    def _(p):
+        lin = lax.rem(me + p, N)
+        pg_copy(lin // G, lax.rem(lin, G)).start()
+
+    decay = -jnp.exp(a_log[at(f, CS, CS), :].T)
+    bias = dt_bias[:, at(f, CS, CS)]
+    gain = skip[:, at(f, CS, CS)]
+    weight = dt_w[:, at(f, CS, CS)]
+    span = STEPS * STATE
+    r_id = lax.broadcasted_iota(jnp.int32, (LANES, 2 * span), 0)
+    q_id = lax.broadcasted_iota(jnp.int32, (LANES, 2 * span), 1)
+    spread = (r_id == (q_id // span) * STATE + q_id % STATE).astype(bf16)
+    own = (
+        lax.broadcasted_iota(jnp.int32, (STEPS, span), 1) // STATE
+        == lax.broadcasted_iota(jnp.int32, (STEPS, span), 0)
+    )
+
+    def scan_block(k, h):
+        for j in range(G):
+            @pl.when(k * G + j != me)
+            def _():
+                there = pg.at[at(k * G + j, R, R)]
+                remote(there, there, pg_ss.at[k * G + j], pg_rs.at[k * G + j], k, j).wait_recv()
+
+        @pl.when(k != f)
+        def _():
+            remote(conv.at[:, at(k, CS, CS)], conv_in.at[k], cv_ss.at[k], cv_rs.at[k], k, c).wait_recv()
+
+        piece = at(k, rows, rows)
+        raw = jnp.dot(pg[piece, :RANK], weight, preferred_element_type=f32) + bias
+        size = jnp.maximum(raw, 0.0) + jnp.log1p(jnp.exp(-jnp.abs(raw)))
+        steps_s[...] = size
+        drive_s[...] = size * conv_in[k].astype(f32)
+        tiled_s[:, : 2 * span] = jnp.dot(pg[piece, RANK:wide], spread, preferred_element_type=f32)
+        tiled_s[:, 2 * span :] = jnp.dot(pg[piece, wide:], spread, preferred_element_type=f32)
+
+        def sub(b, h):
+            sl = at(b, STEPS, STEPS)
+            dt = steps_s[sl]
+            u = drive_s[sl]
+            u_hi = u.astype(bf16)
+            u_lo = (u - u_hi.astype(f32)).astype(bf16)
+
+            def diagonal(i):
+                return jnp.where(own, tiled_s[sl, i * span : (i + 1) * span], 0.0).astype(bf16)
+
+            b_hi, c_hi, b_lo, c_lo = (diagonal(i) for i in range(4))
+            driven = lax.dot_general(
+                jnp.concatenate([b_hi, b_hi, b_lo], axis=0),
+                jnp.concatenate([u_hi, u_lo, u_hi], axis=0),
+                (((0,), (0,)), ((), ())),
+                preferred_element_type=f32,
+            )
+            hs = []
+            for s in range(STEPS):
+                a = jnp.exp(dt[s : s + 1] * decay)
+                h = a * h + driven[s * STATE : (s + 1) * STATE]
+                hs.append(h.astype(bf16))
+            both = jnp.dot(
+                jnp.concatenate([c_hi, c_lo], axis=0),
+                jnp.concatenate(hs, axis=0),
+                preferred_element_type=f32,
+            )
+            y_s[at(k * (rows // STEPS) + b, STEPS, STEPS)] = both[:STEPS] + both[STEPS:]
+            return h
+
+        return lax.fori_loop(0, rows // STEPS, sub, h)
+
+    def scan_and_gate(k, h):
+        h = scan_block(k, h)
+
+        @pl.when(k < F - 1)
+        def _():
+            g = lax.rem(f + 1 + k, F)
+            remote(hidden.at[:, at(g, DB, DB)], hid_in.at[g], hd_ss.at[g], hd_rs.at[g], g, c).wait_recv()
+            gate_block(g)
+
+        return h
+
+    lax.fori_loop(0, F, scan_and_gate, state[at(f, CS, CS), :].T)
+
+    def gated_copy(k, f2):
+        mine = gated.at[at(k, rows, rows), at(f, CS, CS)]
+        return remote(mine, mine, gd_ss.at[k * F + f2], gd_rs.at[k * F + f], f2, c)
+
+    @pl.loop(0, F)
+    def _(k):
+        piece = at(k, rows, rows)
+        pre = gate_own[piece]
+        for j in range(1, F):
+            f2 = lax.rem(f + j, F)
+            remote(
+                gate_send.at[f2, piece], gate_in.at[f2, piece], gt_ss.at[k * F + f2], gt_rs.at[k * F + f2], f2, c
+            ).wait_recv()
+            pre = pre + gate_in[f2, piece].astype(f32)
+        scanned = y_s[piece] + gain * conv_in[k].astype(f32)
+        gated[piece, at(f, CS, CS)] = (scanned * (pre / (1.0 + jnp.exp(-pre)))).astype(bf16)
+        for j in range(1, F):
+            gated_copy(k, lax.rem(f + j, F)).start()
+
+    def out_copy(k, c2):
+        lin = k * G + c2
+        return remote(po.at[at(lin, R, R)], fin_in.at[me], fo_ss.at[lin], fo_rs.at[me], k, c2)
+
+    @pl.loop(0, F)
+    def _(k):
+        piece = at(k, rows, rows)
+        for j in range(1, F):
+            f2 = lax.rem(f + j, F)
+            theirs = gated.at[piece, at(f2, CS, CS)]
+            remote(theirs, theirs, gd_ss.at[k * F + f2], gd_rs.at[k * F + f2], f2, c).wait_recv()
+        po[piece] = lax.dot_general(
+            gated[piece], out_w[...], (((1,), (1,)), ((), ())), preferred_element_type=f32
+        ).astype(bf16)
+        for j in range(G):
+            c2 = lax.rem(c + j, G)
+            if j == 0:
+                pl.when(k != f)(lambda: out_copy(k, c2).start())
+            else:
+                out_copy(k, c2).start()
+
+    fin_in[me] = po[at(me, R, R)]
+    for f2 in range(F):
+        total = jnp.zeros((R, DB), f32)
+        for c2 in range(G):
+            lin = f2 * G + c2
+
+            @pl.when(lin != me)
+            def _():
+                remote(po.at[at(lin, R, R)], fin_in.at[lin], fo_ss.at[lin], fo_rs.at[lin], f2, c2).wait_recv()
+
+            total = total + fin_in[lin].astype(f32)
+        out[:, f2 * DB : (f2 + 1) * DB] = total.astype(bf16)
+
+    pl.loop(1, G)(lambda j: pp_copy(j).wait_send())
+    for j in range(1, F):
+        f2 = lax.rem(f + j, F)
+        hid_copy(f2).wait_send()
+        conv_copy(f2).wait_send()
+
+        @pl.loop(0, F)
+        def _(k):
+            gate_copy(k, f2).wait_send()
+            gated_copy(k, f2).wait_send()
+
+    @pl.loop(1, N)
+    def _(p):
+        lin = lax.rem(me + p, N)
+        pg_copy(lin // G, lax.rem(lin, G)).wait_send()
+        out_copy(lin // G, lax.rem(lin, G)).wait_send()
+
+
+def shards(F, G, *args):
+    hidden, conv_out, state_in, gate_weight, xproj_weight, dt_weight, dt_bias, a_log, skip_gain, out_weight = args
+    rows, channels = conv_out.shape
+    depth, width = gate_weight.shape[0], hidden.shape[1]
+    if rows % (16 * G) or channels % (LANES * F) or depth % LANES or width != depth * F:
+        return generic_shards(*args)
+    f32, bf16 = jnp.float32, jnp.bfloat16
+    N, R, CS, L = F * G, rows // G, channels // F, rows * F
+    wide = RANK + LANES
+    span = STEPS * STATE
+    dma = pltpu.SemaphoreType.DMA
+    scratch = [
+        pltpu.VMEM((rows, wide), f32),
+        pltpu.VMEM((G, R, wide), f32),
+        pltpu.VMEM((F, rows, CS), bf16),
+        pltpu.VMEM((F, rows, depth), bf16),
+        pltpu.VMEM((L, wide + LANES), bf16),
+        pltpu.VMEM((F, L, CS), bf16),
+        pltpu.VMEM((L, CS), f32),
+        pltpu.VMEM((F, L, CS), bf16),
+        pltpu.VMEM((rows, CS), f32),
+        pltpu.VMEM((rows, CS), f32),
+        pltpu.VMEM((rows, 4 * span), f32),
+        pltpu.VMEM((L, CS), f32),
+        pltpu.VMEM((L, channels), bf16),
+        pltpu.VMEM((L, depth), bf16),
+        pltpu.VMEM((N, R, depth), bf16),
+    ]
+    for count in (G, F, F, N, F * F, F * F, N):
+        scratch += [dma((count,)), dma((count,))]
+    return pl.pallas_call(
+        functools.partial(fused_kernel, F, G),
+        out_shape=jax.ShapeDtypeStruct((R, width), bf16),
+        in_specs=[pl.BlockSpec(memory_space=pltpu.VMEM)] * 10,
+        out_specs=pl.BlockSpec(memory_space=pltpu.VMEM),
+        scratch_shapes=scratch,
+        compiler_params=pltpu.CompilerParams(
+            collective_id=0, has_side_effects=True, vmem_limit_bytes=48 * 2**20
+        ),
+    )(
+        hidden,
+        conv_out,
+        state_in,
+        gate_weight,
+        xproj_weight,
+        dt_weight,
+        dt_bias[None],
+        a_log,
+        skip_gain[None],
+        out_weight,
+    )
 
 
 def solution(mesh):
@@ -121,5 +473,5 @@
         P("fsdp", "chan"),
     )
     return jax.shard_map(
-        shards, mesh=mesh, in_specs=placed, out_specs=P(("fsdp", "chan"), None), check_vma=False
-    )
+        functools.partial(shards, mesh.shape["fsdp"], mesh.shape["chan"]), mesh=mesh, in_specs=placed, out_specs=P(("fsdp", "chan"), None), check_vma=False
+    )

time: 406 us -> 93.4 us (0.23)
  the two profiles are of different devices: /device:TPU:0 before, /device:TPU:27 now
where the time goes in v1:
time: 93.4 us; the launch traced here: 93 us
  Pallas kernels  83.6 us (90%)
  local copies, waits for them, and re-layouts  9.36 us (10%)
    pallas_call x1, Pallas kernels, shards(): pl.pallas_call(functools.partial(fused_kernel, F, G), out_shape=jax.Shape...  83.6 us
    unnamed x18, local copies, waits for them, and re-layouts  9.36 us

profile of v1, /device:TPU:27, one launch (start us, length us, event | category | flops | bytes accessed | tf_op | source)
XLA Modules:
  0.0 93.0 jit_solution(5207924359990211167)
XLA Ops:
  0.0 0.0 copy-start.6
  0.0 0.0 copy-start.5
  0.0 0.0 copy-start
  0.0 1.2 %copy.11.state = f32[1024,16]{1,0:T(8,128)S(1)} copy(f32[1024,16]{0,1:T(8,128)} %param.12) | data formatting | bytes 131072 | tf_op args[2]
  1.2 1.8 %copy.13.a_log = f32[1024,16]{1,0:T(8,128)} copy(f32[1024,16]{0,1:T(8,128)} %param.17) | data formatting | bytes 131072 | tf_op args[7]
  3.0 1.4 %copy.12.xproj = bf16[1024,288]{1,0:T(8,128)(2,1)S(1)} copy(bf16[1024,288]{0,1:T(8,128)(2,1)} %param.14) | data formatting | bytes 1179648 | tf_op args[4]
  4.5 0.0 copy-done.6
  4.5 0.0 copy-done.5
  4.5 0.0 copy-done
  4.5 0.0 copy-start.1
  4.5 1.0 %copy-done.1 = f32[1024,16]{1,0:T(8,128)S(1)} copy-done((f32[1024,16]{1,0:T(8,128)S(1)}, f32[1024,16]{1,0:T(8,128)}, u32[]{:S(2)}) %copy-start.1) | copy-done | bytes 65560
  5.5 0.0 copy-start.2
  5.5 1.2 %copy-done.2 = bf16[128,4096]{1,0:T(8,128)(2,1)S(1)} copy-done((bf16[128,4096]{1,0:T(8,128)(2,1)S(1)}, bf16[128,4096]{1,0:T(8,128)(2,1)}, u32[]{:S(2)}) %copy-start.2) | copy-done | bytes 1048600
  6.8 0.0 copy-start.3
  6.8 1.0 %copy-done.3 = bf16[256,1024]{1,0:T(8,128)(2,1)S(1)} copy-done((bf16[256,1024]{1,0:T(8,128)(2,1)S(1)}, bf16[256,1024]{1,0:T(8,128)(2,1)}, u32[]{:S(2)}) %copy-start.3) | copy-done | bytes 524312
  7.8 0.0 copy-start.4
  7.8 0.9 %copy-done.4 = bf16[128,1024]{1,0:T(8,128)(2,1)S(1)} copy-done((bf16[128,1024]{1,0:T(8,128)(2,1)S(1)}, bf16[128,1024]{1,0:T(8,128)(2,1)}, u32[]{:S(2)}) %copy-start.4) | copy-done | bytes 262168
  8.8 83.6 %shard_map.100 = bf16[16,4096]{1,0:T(8,128)(2,1)S(1)} custom-call(bf16[128,4096]{1,0:T(8,128)(2,1)S(1)} %copy-done.2, bf16[128,1024]{1,0:T(8,128)(2,1)S(1)} %copy-done.4, f32[1024,16]{1,0:T(8,128)S(1)} %copy.11.state, bf16[1024,1024]{1,0:T(8,128)(2,1)S(1)} %copy-done, bf16[1024,288]{1,0:T(8,128)(2,1)S(1)} %copy.12.xproj, bf16[256,1024]{1,0:T(8,128)(2,1)S(1)} %copy-done.3, ...), custom_call_target="tpu_custom_call" | custom-call | tf_op jit(solution)/shard_map/pallas_call | solution.py:439
  92.4 0.7 copy.15
Async XLA Ops:
  0.0 4.5 %copy-start.6 = (f32[1024]{0:T(1024)S(1)}, f32[1024]{0:T(1024)}, u32[]{:S(2)}) copy-start(f32[1024]{0:T(1024)} %param.18) | copy-start | bytes 12292
  0.0 4.5 %copy-start.5 = (f32[1024]{0:T(1024)S(1)}, f32[1024]{0:T(1024)}, u32[]{:S(2)}) copy-start(f32[1024]{0:T(1024)} %param.16) | copy-start | bytes 12292
  0.0 4.5 %copy-start = (bf16[1024,1024]{1,0:T(8,128)(2,1)S(1)}, bf16[1024,1024]{1,0:T(8,128)(2,1)}, u32[]{:S(2)}) copy-start(bf16[1024,1024]{1,0:T(8,128)(2,1)} %gate_w.1) | copy-start | bytes 6291460
  4.5 1.0 %copy-start.1 = (f32[1024,16]{1,0:T(8,128)S(1)}, f32[1024,16]{1,0:T(8,128)}, u32[]{:S(2)}) copy-start(f32[1024,16]{1,0:T(8,128)} %copy.13.a_log) | copy-start | bytes 196612
  5.5 1.2 %copy-start.2 = (bf16[128,4096]{1,0:T(8,128)(2,1)S(1)}, bf16[128,4096]{1,0:T(8,128)(2,1)}, u32[]{:S(2)}) copy-start(bf16[128,4096]{1,0:T(8,128)(2,1)} %hidden.1) | copy-start | bytes 3145732
  6.8 1.0 %copy-start.3 = (bf16[256,1024]{1,0:T(8,128)(2,1)S(1)}, bf16[256,1024]{1,0:T(8,128)(2,1)}, u32[]{:S(2)}) copy-start(bf16[256,1024]{1,0:T(8,128)(2,1)} %dt_w.1) | copy-start | bytes 1572868
  7.8 0.9 %copy-start.4 = (bf16[128,1024]{1,0:T(8,128)(2,1)S(1)}, bf16[128,1024]{1,0:T(8,128)(2,1)}, u32[]{:S(2)}) copy-start(bf16[128,1024]{1,0:T(8,128)(2,1)} %conv.1) | copy-start | bytes 786436

commit v2 on v1

--- a/solution.py
+++ b/solution.py
@@ -124,16 +124,24 @@
     F,
     G,
     hidden,
+    conv_h,
+    state_h,
+    gate_h,
+    xproj_h,
+    dt_h,
+    dt_bias,
+    a_log_h,
+    skip,
+    out_h,
+    out,
     conv,
     state,
     gate_w,
     xproj,
     dt_w,
-    dt_bias,
     a_log,
-    skip,
     out_w,
-    out,
+    load_sem,
     pp,
     pp_in,
     conv_in,
@@ -148,7 +156,11 @@
     y_s,
     gated,
     po,
-    fin_in,
+    ya_in,
+    pair,
+    zb_in,
+    done,
+    fc_in,
     pp_ss,
     pp_rs,
     cv_ss,
@@ -157,12 +169,19 @@
     hd_rs,
     pg_ss,
     pg_rs,
+    pb_ss,
+    pb_rs,
     gt_ss,
     gt_rs,
     gd_ss,
     gd_rs,
-    fo_ss,
-    fo_rs,
+    gf_ss,
+    ya_ss,
+    ya_rs,
+    zb_ss,
+    zb_rs,
+    fc_ss,
+    fc_rs,
 ):
     f32, bf16 = jnp.float32, jnp.bfloat16
     N = F * G
@@ -170,6 +189,10 @@
     me = f * G + c
     rows, channels = conv.shape
     R, CS, DB = rows // G, channels // F, gate_w.shape[0]
+    H = G // 2
+    mate = f + 1 - 2 * lax.rem(f, 2)
+    c_mate = c + 1 - 2 * lax.rem(c, 2)
+    peers = [lax.rem(f + j, F) for j in range(2, F, 2)]
     wide = pp.shape[1]
 
     def remote(src, dst, ss, rs, f2, c2):
@@ -185,6 +208,24 @@
     def at(base, size, step):
         return pl.ds(pl.multiple_of(base * step, step), size)
 
+    mine = at(f, CS, CS)
+    loads = [
+        pltpu.make_async_copy(src, dst, load_sem.at[i])
+        for i, (src, dst) in enumerate(
+            (
+                (conv_h, conv),
+                (xproj_h, xproj),
+                (hidden.at[:, at(f, DB, DB)], hid_in.at[f]),
+                (gate_h, gate_w),
+                (dt_h.at[:, mine], dt_w),
+                (a_log_h.at[:, mine], a_log),
+                (state_h.at[:, mine], state),
+                (out_h, out_w),
+            )
+        )
+    ]
+    for load in loads:
+        load.start()
     barrier = pltpu.get_barrier_semaphore()
 
     @pl.loop(1, N)
@@ -198,7 +239,11 @@
         )
 
     pp[:, RANK:] = jnp.zeros((rows, wide - RANK), f32)
-    pp[:, : xproj.shape[1]] = jnp.dot(conv[...], xproj[...], preferred_element_type=f32)
+    loads[0].wait()
+    loads[1].wait()
+    pp[:, : xproj.shape[0]] = lax.dot_general(
+        conv[...], xproj[...], (((1,), (1,)), ((), ())), preferred_element_type=f32
+    )
     pl.semaphore_wait(barrier, N - 1)
 
     def pp_copy(j):
@@ -216,7 +261,8 @@
         hid_copy(lax.rem(f + j, F)).start()
         conv_copy(lax.rem(f + j, F)).start()
     conv_in[f] = conv[:, at(f, CS, CS)]
-    hid_in[f] = hidden[:, at(f, DB, DB)]
+    loads[2].wait()
+    loads[3].wait()
 
     def gate_copy(k, f2):
         piece = at(k, rows, rows)
@@ -245,26 +291,39 @@
         total = total + pp_in[c2]
     high = total.astype(bf16)
     low = (total[:, RANK:] - high[:, RANK:].astype(f32)).astype(bf16)
-    pg[at(me, R, R), :wide] = high
-    pg[at(me, R, R), wide:] = low
-
-    def pg_copy(f2, c2):
-        mine = pg.at[at(me, R, R)]
-        lin = f2 * G + c2
-        return remote(mine, mine, pg_ss.at[lin], pg_rs.at[me], f2, c2)
-
-    @pl.loop(1, N)
-    def _(p):
-        lin = lax.rem(me + p, N)
-        pg_copy(lin // G, lax.rem(lin, G)).start()
-
-    decay = -jnp.exp(a_log[at(f, CS, CS), :].T)
+    used = xproj.shape[0]
+    pg[at(me, R, R)] = jnp.concatenate(
+        [high[:, :used], low[:, : used - RANK], jnp.zeros((R, wide - 2 * used + RANK), bf16)], axis=1
+    )
+
+    def pg_copy(c2):
+        rows_of = pg.at[at(me, R, R)]
+        return remote(rows_of, rows_of, pg_ss.at[c2], pg_rs.at[c], f, c2)
+
+    def pg_block(f2):
+        rows_of = pg.at[at(f, rows, rows)]
+        return remote(rows_of, rows_of, pb_ss.at[f2], pb_rs.at[f], f2, c)
+
+    pl.loop(1, G)(lambda j: pg_copy(lax.rem(c + j, G)).start())
+
+    @pl.loop(1, G)
+    def _(j):
+        c2 = lax.rem(c + j, G)
+        there = pg.at[at(f * G + c2, R, R)]
+        remote(there, there, pg_ss.at[c2], pg_rs.at[c2], f, c2).wait_recv()
+
+    for j in range(1, F):
+        pg_block(lax.rem(f + j, F)).start()
+    for load in loads[4:]:
+        load.wait()
+
+    decay = -jnp.exp(a_log[...])
     bias = dt_bias[:, at(f, CS, CS)]
     gain = skip[:, at(f, CS, CS)]
-    weight = dt_w[:, at(f, CS, CS)]
+    weight = dt_w[...]
     span = STEPS * STATE
-    r_id = lax.broadcasted_iota(jnp.int32, (LANES, 2 * span), 0)
-    q_id = lax.broadcasted_iota(jnp.int32, (LANES, 2 * span), 1)
+    r_id = lax.broadcasted_iota(jnp.int32, (LANES, 4 * span), 0)
+    q_id = lax.broadcasted_iota(jnp.int32, (LANES, 4 * span), 1)
     spread = (r_id == (q_id // span) * STATE + q_id % STATE).astype(bf16)
     own = (
         lax.broadcasted_iota(jnp.int32, (STEPS, span), 1) // STATE
@@ -272,14 +331,10 @@
     )
 
     def scan_block(k, h):
-        for j in range(G):
-            @pl.when(k * G + j != me)
-            def _():
-                there = pg.at[at(k * G + j, R, R)]
-                remote(there, there, pg_ss.at[k * G + j], pg_rs.at[k * G + j], k, j).wait_recv()
-
         @pl.when(k != f)
         def _():
+            there = pg.at[at(k, rows, rows)]
+            remote(there, there, pb_ss.at[k], pb_rs.at[k], k, c).wait_recv()
             remote(conv.at[:, at(k, CS, CS)], conv_in.at[k], cv_ss.at[k], cv_rs.at[k], k, c).wait_recv()
 
         piece = at(k, rows, rows)
@@ -287,8 +342,7 @@
         size = jnp.maximum(raw, 0.0) + jnp.log1p(jnp.exp(-jnp.abs(raw)))
         steps_s[...] = size
         drive_s[...] = size * conv_in[k].astype(f32)
-        tiled_s[:, : 2 * span] = jnp.dot(pg[piece, RANK:wide], spread, preferred_element_type=f32)
-        tiled_s[:, 2 * span :] = jnp.dot(pg[piece, wide:], spread, preferred_element_type=f32)
+        tiled_s[...] = jnp.dot(pg[piece, RANK:], spread, preferred_element_type=f32)
 
         def sub(b, h):
             sl = at(b, STEPS, STEPS)
@@ -333,7 +387,7 @@
 
         return h
 
-    lax.fori_loop(0, F, scan_and_gate, state[at(f, CS, CS), :].T)
+    lax.fori_loop(0, F, scan_and_gate, state[...])
 
     def gated_copy(k, f2):
         mine = gated.at[at(k, rows, rows), at(f, CS, CS)]
@@ -351,42 +405,78 @@
             pre = pre + gate_in[f2, piece].astype(f32)
         scanned = y_s[piece] + gain * conv_in[k].astype(f32)
         gated[piece, at(f, CS, CS)] = (scanned * (pre / (1.0 + jnp.exp(-pre)))).astype(bf16)
-        for j in range(1, F):
-            gated_copy(k, lax.rem(f + j, F)).start()
-
-    def out_copy(k, c2):
-        lin = k * G + c2
-        return remote(po.at[at(lin, R, R)], fin_in.at[me], fo_ss.at[lin], fo_rs.at[me], k, c2)
-
-    @pl.loop(0, F)
+        for f2 in [mate] + peers:
+            gated_copy(k, f2).start()
+
+    def forward(k, f2):
+        theirs = gated.at[at(k, rows, rows), at(f2, CS, CS)]
+        return remote(theirs, theirs, gf_ss.at[k * F + f2], gd_rs.at[k * F + f2], mate, c)
+
+    def gated_wait(k, f2):
+        theirs = gated.at[at(k, rows, rows), at(f2, CS, CS)]
+        remote(theirs, theirs, gd_ss.at[k * F + f2], gd_rs.at[k * F + f2], f2, c).wait_recv()
+
+    def pass_on(k):
+        for f2 in peers:
+            gated_wait(k, f2)
+            forward(k, f2).start()
+
+    half, mine_z = lax.rem(c, 2), c // 2
+
+    def ya_copy(k):
+        return remote(po.at[k, :, 1 - half], ya_in.at[k], ya_ss.at[k], ya_rs.at[k], f, c_mate)
+
+    def zb_copy(k, z):
+        return remote(pair.at[k, z], zb_in.at[k, mine_z], zb_ss.at[k * H + z], zb_rs.at[k * H + mine_z], f, 2 * z + half)
+
+    def fc_copy(k):
+        return remote(done.at[k], fc_in.at[f], fc_ss.at[k], fc_rs.at[f], k, c)
+
+    pass_on(0)
+
+    @pl.loop(0, F + 2)
     def _(k):
-        piece = at(k, rows, rows)
-        for j in range(1, F):
-            f2 = lax.rem(f + j, F)
-            theirs = gated.at[piece, at(f2, CS, CS)]
-            remote(theirs, theirs, gd_ss.at[k * F + f2], gd_rs.at[k * F + f2], f2, c).wait_recv()
-        po[piece] = lax.dot_general(
-            gated[piece], out_w[...], (((1,), (1,)), ((), ())), preferred_element_type=f32
-        ).astype(bf16)
-        for j in range(G):
-            c2 = lax.rem(c + j, G)
-            if j == 0:
-                pl.when(k != f)(lambda: out_copy(k, c2).start())
-            else:
-                out_copy(k, c2).start()
-
-    fin_in[me] = po[at(me, R, R)]
+        @pl.when(k + 1 < F)
+        def _():
+            pass_on(k + 1)
+
+        @pl.when(k < F)
+        def _():
+            gated_wait(k, mate)
+            for j in range(2, F, 2):
+                gated_wait(k, lax.rem(mate + j, F))
+            part = lax.dot_general(
+                gated[at(k, rows, rows)], out_w[...], (((1,), (1,)), ((), ())), preferred_element_type=f32
+            )
+            po[k] = part.astype(bf16).reshape(H, 2, R, DB)
+            ya_copy(k).start()
+
+        @pl.when((k >= 1) & (k < F + 1))
+        def _():
+            q = k - 1
+            ya_copy(q).wait_recv()
+            pair[q] = (po[q, :, half].astype(f32) + ya_in[q].astype(f32)).astype(bf16)
+            for j in range(1, H):
+                zb_copy(q, lax.rem(mine_z + j, H)).start()
+
+        @pl.when(k >= 2)
+        def _():
+            q = k - 2
+            total = pair[q, mine_z].astype(f32)
+            for j in range(1, H):
+                z = lax.rem(mine_z + j, H)
+                remote(pair.at[q, z], zb_in.at[q, z], zb_ss.at[q * H + z], zb_rs.at[q * H + z], f, 2 * z + half).wait_recv()
+                total = total + zb_in[q, z].astype(f32)
+            done[q] = total.astype(bf16)
+            pl.when(q != f)(lambda: fc_copy(q).start())
+
+    fc_in[f] = done[f]
     for f2 in range(F):
-        total = jnp.zeros((R, DB), f32)
-        for c2 in range(G):
-            lin = f2 * G + c2
-
-            @pl.when(lin != me)
-            def _():
-                remote(po.at[at(lin, R, R)], fin_in.at[lin], fo_ss.at[lin], fo_rs.at[lin], f2, c2).wait_recv()
-
-            total = total + fin_in[lin].astype(f32)
-        out[:, f2 * DB : (f2 + 1) * DB] = total.astype(bf16)
+        @pl.when(f2 != f)
+        def _():
+            remote(done.at[f2], fc_in.at[f2], fc_ss.at[f2], fc_rs.at[f2], f2, c).wait_recv()
+
+        out[:, f2 * DB : (f2 + 1) * DB] = fc_in[f2]
 
     pl.loop(1, G)(lambda j: pp_copy(j).wait_send())
     for j in range(1, F):
@@ -397,32 +487,49 @@
         @pl.loop(0, F)
         def _(k):
             gate_copy(k, f2).wait_send()
+
+        pg_block(f2).wait_send()
+        fc_copy(f2).wait_send()
+
+    @pl.loop(0, F)
+    def _(k):
+        gated_copy(k, mate).wait_send()
+        for f2 in peers:
             gated_copy(k, f2).wait_send()
-
-    @pl.loop(1, N)
-    def _(p):
-        lin = lax.rem(me + p, N)
-        pg_copy(lin // G, lax.rem(lin, G)).wait_send()
-        out_copy(lin // G, lax.rem(lin, G)).wait_send()
+            forward(k, f2).wait_send()
+        ya_copy(k).wait_send()
+        for j in range(1, H):
+            zb_copy(k, lax.rem(mine_z + j, H)).wait_send()
+
+    pl.loop(1, G)(lambda j: pg_copy(lax.rem(c + j, G)).wait_send())
 
 
 def shards(F, G, *args):
     hidden, conv_out, state_in, gate_weight, xproj_weight, dt_weight, dt_bias, a_log, skip_gain, out_weight = args
     rows, channels = conv_out.shape
     depth, width = gate_weight.shape[0], hidden.shape[1]
-    if rows % (16 * G) or channels % (LANES * F) or depth % LANES or width != depth * F:
+    if G % 2 or F % 2 or rows % (16 * G) or channels % (LANES * F) or depth % LANES or width != depth * F:
         return generic_shards(*args)
     f32, bf16 = jnp.float32, jnp.bfloat16
-    N, R, CS, L = F * G, rows // G, channels // F, rows * F
+    R, CS, L = rows // G, channels // F, rows * F
     wide = RANK + LANES
     span = STEPS * STATE
     dma = pltpu.SemaphoreType.DMA
+    H = G // 2
     scratch = [
+        pltpu.VMEM((rows, channels), bf16),
+        pltpu.VMEM((STATE, CS), f32),
+        pltpu.VMEM((depth, channels), bf16),
+        pltpu.VMEM((xproj_weight.shape[1], channels), bf16),
+        pltpu.VMEM((RANK, CS), bf16),
+        pltpu.VMEM((STATE, CS), f32),
+        pltpu.VMEM((depth, channels), bf16),
+        dma((8,)),
         pltpu.VMEM((rows, wide), f32),
         pltpu.VMEM((G, R, wide), f32),
         pltpu.VMEM((F, rows, CS), bf16),
         pltpu.VMEM((F, rows, depth), bf16),
-        pltpu.VMEM((L, wide + LANES), bf16),
+        pltpu.VMEM((L, wide), bf16),
         pltpu.VMEM((F, L, CS), bf16),
         pltpu.VMEM((L, CS), f32),
         pltpu.VMEM((F, L, CS), bf16),
@@ -431,15 +538,23 @@
         pltpu.VMEM((rows, 4 * span), f32),
         pltpu.VMEM((L, CS), f32),
         pltpu.VMEM((L, channels), bf16),
-        pltpu.VMEM((L, depth), bf16),
-        pltpu.VMEM((N, R, depth), bf16),
+        pltpu.VMEM((F, H, 2, R, depth), bf16),
+        pltpu.VMEM((F, H, R, depth), bf16),
+        pltpu.VMEM((F, H, R, depth), bf16),
+        pltpu.VMEM((F, H, R, depth), bf16),
+        pltpu.VMEM((F, R, depth), bf16),
+        pltpu.VMEM((F, R, depth), bf16),
     ]
-    for count in (G, F, F, N, F * F, F * F, N):
+    for count in (G, F, F, G, F, F * F, F * F):
         scratch += [dma((count,)), dma((count,))]
+    scratch.append(dma((F * F,)))
+    for count in (F, F * H, F):
+        scratch += [dma((count,)), dma((count,))]
+    in_vmem, in_hbm = pl.BlockSpec(memory_space=pltpu.VMEM), pl.BlockSpec(memory_space=pltpu.HBM)
     return pl.pallas_call(
         functools.partial(fused_kernel, F, G),
         out_shape=jax.ShapeDtypeStruct((R, width), bf16),
-        in_specs=[pl.BlockSpec(memory_space=pltpu.VMEM)] * 10,
+        in_specs=[in_hbm] * 6 + [in_vmem, in_hbm, in_vmem, in_hbm],
         out_specs=pl.BlockSpec(memory_space=pltpu.VMEM),
         scratch_shapes=scratch,
         compiler_params=pltpu.CompilerParams(
@@ -448,12 +563,12 @@
     )(
         hidden,
         conv_out,
-        state_in,
+        state_in.T,
         gate_weight,
-        xproj_weight,
+        xproj_weight.T,
         dt_weight,
         dt_bias[None],
-        a_log,
+        a_log.T,
         skip_gain[None],
         out_weight,
     )

time: 93.4 us -> 83.8 us (0.90)
  the two profiles are of different devices: /device:TPU:27 before, /device:TPU:0 now
where the time goes in v2:
time: 83.8 us; the launch traced here: 83.4 us
  Pallas kernels  73.8 us (88%)
  local copies, waits for them, and re-layouts  9.58 us (11%)
    pallas_call x1, Pallas kernels, shards(): pl.pallas_call(functools.partial(fused_kernel, F, G), out_shape=jax.Shape...  73.8 us
    unnamed x19, local copies, waits for them, and re-layouts  9.58 us

profile of v2, /device:TPU:0, one launch (start us, length us, event | category | flops | bytes accessed | tf_op | source)
XLA Modules:
  0.0 83.4 jit_solution(9169793381719910899)
XLA Ops:
  0.0 0.0 copy-start
  0.0 1.6 %copy-done = bf16[1024,1024]{1,0:T(8,128)(2,1)S(1)} copy-done((bf16[1024,1024]{1,0:T(8,128)(2,1)S(1)}, bf16[1024,1024]{1,0:T(8,128)(2,1)}, u32[]{:S(2)}) %copy-start) | copy-done | bytes 2097176
  1.6 0.0 copy-start.1
  1.6 1.2 %copy-done.1 = bf16[128,4096]{1,0:T(8,128)(2,1)S(1)} copy-done((bf16[128,4096]{1,0:T(8,128)(2,1)S(1)}, bf16[128,4096]{1,0:T(8,128)(2,1)}, u32[]{:S(2)}) %copy-start.1) | copy-done | bytes 1048600
  2.8 0.0 copy-start.2
  2.8 1.1 %copy-done.2 = bf16[1024,288]{0,1:T(8,128)(2,1)S(1)} copy-done((bf16[1024,288]{0,1:T(8,128)(2,1)S(1)}, bf16[1024,288]{0,1:T(8,128)(2,1)}, u32[]{:S(2)}) %copy-start.2) | copy-done | bytes 589848
  3.9 0.0 copy-start.3
  3.9 1.0 %copy-done.3 = bf16[256,1024]{1,0:T(8,128)(2,1)S(1)} copy-done((bf16[256,1024]{1,0:T(8,128)(2,1)S(1)}, bf16[256,1024]{1,0:T(8,128)(2,1)}, u32[]{:S(2)}) %copy-start.3) | copy-done | bytes 524312
  4.9 0.0 copy-start.4
  4.9 0.9 %copy-done.4 = bf16[128,1024]{1,0:T(8,128)(2,1)S(1)} copy-done((bf16[128,1024]{1,0:T(8,128)(2,1)S(1)}, bf16[128,1024]{1,0:T(8,128)(2,1)}, u32[]{:S(2)}) %copy-start.4) | copy-done | bytes 262168
  5.9 0.0 copy-start.5
  5.9 0.8 %copy-done.5 = f32[1024,16]{0,1:T(8,128)S(1)} copy-done((f32[1024,16]{0,1:T(8,128)S(1)}, f32[1024,16]{0,1:T(8,128)}, u32[]{:S(2)}) %copy-start.5) | copy-done | bytes 65560
  6.7 0.0 copy-start.6
  6.7 0.8 %copy-done.6 = f32[1024,16]{0,1:T(8,128)S(1)} copy-done((f32[1024,16]{0,1:T(8,128)S(1)}, f32[1024,16]{0,1:T(8,128)}, u32[]{:S(2)}) %copy-start.6) | copy-done | bytes 65560
  7.6 0.0 copy-start.7
  7.6 0.7 copy-done.7
  8.2 0.0 copy-start.8
  8.2 0.7 copy-done.8
  8.9 73.8 %shard_map.100 = bf16[16,4096]{1,0:T(8,128)(2,1)S(1)} custom-call(bf16[128,4096]{1,0:T(8,128)(2,1)S(1)} %copy-done.1, bf16[128,1024]{1,0:T(8,128)(2,1)S(1)} %copy-done.4, f32[16,1024]{1,0:T(8,128)S(1)} %bitcast.6, bf16[1024,1024]{1,0:T(8,128)(2,1)S(1)} %copy-done, bf16[288,1024]{1,0:T(8,128)(2,1)S(1)} %bitcast.5, bf16[256,1024]{1,0:T(8,128)(2,1)S(1)} %copy-done.3, ...), custom_call_target="tpu_custom_call" | custom-call | tf_op jit(solution)/shard_map/pallas_call | solution.py:554
  82.7 0.7 copy.12
Async XLA Ops:
  0.0 1.6 %copy-start = (bf16[1024,1024]{1,0:T(8,128)(2,1)S(1)}, bf16[1024,1024]{1,0:T(8,128)(2,1)}, u32[]{:S(2)}) copy-start(bf16[1024,1024]{1,0:T(8,128)(2,1)} %gate_h.1) | copy-start | bytes 6291460
  1.6 1.2 %copy-start.1 = (bf16[128,4096]{1,0:T(8,128)(2,1)S(1)}, bf16[128,4096]{1,0:T(8,128)(2,1)}, u32[]{:S(2)}) copy-start(bf16[128,4096]{1,0:T(8,128)(2,1)} %hidden.1) | copy-start | bytes 3145732
  2.8 1.1 %copy-start.2 = (bf16[1024,288]{0,1:T(8,128)(2,1)S(1)}, bf16[1024,288]{0,1:T(8,128)(2,1)}, u32[]{:S(2)}) copy-start(bf16[1024,288]{0,1:T(8,128)(2,1)} %param.14) | copy-start | bytes 1769476
  3.9 1.0 %copy-start.3 = (bf16[256,1024]{1,0:T(8,128)(2,1)S(1)}, bf16[256,1024]{1,0:T(8,128)(2,1)}, u32[]{:S(2)}) copy-start(bf16[256,1024]{1,0:T(8,128)(2,1)} %dt_h.1) | copy-start | bytes 1572868
  4.9 0.9 %copy-start.4 = (bf16[128,1024]{1,0:T(8,128)(2,1)S(1)}, bf16[128,1024]{1,0:T(8,128)(2,1)}, u32[]{:S(2)}) copy-start(bf16[128,1024]{1,0:T(8,128)(2,1)} %conv_h.1) | copy-start | bytes 786436
  5.9 0.8 %copy-start.5 = (f32[1024,16]{0,1:T(8,128)S(1)}, f32[1024,16]{0,1:T(8,128)}, u32[]{:S(2)}) copy-start(f32[1024,16]{0,1:T(8,128)} %param.12) | copy-start | bytes 196612
  6.7 0.8 %copy-start.6 = (f32[1024,16]{0,1:T(8,128)S(1)}, f32[1024,16]{0,1:T(8,128)}, u32[]{:S(2)}) copy-start(f32[1024,16]{0,1:T(8,128)} %param.17) | copy-start | bytes 196612
  7.6 0.7 copy-start.7
  8.2 0.7 copy-start.8

commit v3 on v2

--- a/solution.py
+++ b/solution.py
@@ -118,6 +118,7 @@
 
 LANES = 128
 STEPS = 16
+LAGS = (0, 1, 1, 2, 3)
 
 
 def fused_kernel(
@@ -184,7 +185,6 @@
     fc_rs,
 ):
     f32, bf16 = jnp.float32, jnp.bfloat16
-    N = F * G
     f, c = lax.axis_index("fsdp"), lax.axis_index("chan")
     me = f * G + c
     rows, channels = conv.shape
@@ -193,6 +193,7 @@
     mate = f + 1 - 2 * lax.rem(f, 2)
     c_mate = c + 1 - 2 * lax.rem(c, 2)
     peers = [lax.rem(f + j, F) for j in range(2, F, 2)]
+    mates = [lax.rem(mate + j, F) for j in range(2, F, 2)]
     wide = pp.shape[1]
 
     def remote(src, dst, ss, rs, f2, c2):
@@ -228,23 +229,21 @@
         load.start()
     barrier = pltpu.get_barrier_semaphore()
 
-    @pl.loop(1, N)
-    def _(p):
-        lin = lax.rem(me + p, N)
-        pl.semaphore_signal(
-            barrier,
-            inc=1,
-            device_id={"fsdp": lin // G, "chan": lax.rem(lin, G)},
-            device_id_type=pl.DeviceIdType.MESH,
-        )
-
-    pp[:, RANK:] = jnp.zeros((rows, wide - RANK), f32)
+    @pl.loop(1, G)
+    def _(j):
+        there = {"fsdp": f, "chan": lax.rem(c + j, G)}
+        pl.semaphore_signal(barrier, inc=1, device_id=there, device_id_type=pl.DeviceIdType.MESH)
+
+    for j in range(1, F):
+        there = {"fsdp": lax.rem(f + j, F), "chan": c}
+        pl.semaphore_signal(barrier, inc=1, device_id=there, device_id_type=pl.DeviceIdType.MESH)
+
     loads[0].wait()
     loads[1].wait()
     pp[:, : xproj.shape[0]] = lax.dot_general(
         conv[...], xproj[...], (((1,), (1,)), ((), ())), preferred_element_type=f32
     )
-    pl.semaphore_wait(barrier, N - 1)
+    pl.semaphore_wait(barrier, G + F - 2)
 
     def pp_copy(j):
         c2 = lax.rem(c + j, G)
@@ -314,6 +313,9 @@
 
     for j in range(1, F):
         pg_block(lax.rem(f + j, F)).start()
+    for g in [mate] + peers + mates:
+        remote(hidden.at[:, at(g, DB, DB)], hid_in.at[g], hd_ss.at[g], hd_rs.at[g], g, c).wait_recv()
+        gate_block(g)
     for load in loads[4:]:
         load.wait()
 
@@ -376,25 +378,35 @@
 
         return lax.fori_loop(0, rows // STEPS, sub, h)
 
-    def scan_and_gate(k, h):
-        h = scan_block(k, h)
-
-        @pl.when(k < F - 1)
-        def _():
-            g = lax.rem(f + 1 + k, F)
-            remote(hidden.at[:, at(g, DB, DB)], hid_in.at[g], hd_ss.at[g], hd_rs.at[g], g, c).wait_recv()
-            gate_block(g)
-
-        return h
-
-    lax.fori_loop(0, F, scan_and_gate, state[...])
-
     def gated_copy(k, f2):
         mine = gated.at[at(k, rows, rows), at(f, CS, CS)]
         return remote(mine, mine, gd_ss.at[k * F + f2], gd_rs.at[k * F + f], f2, c)
 
-    @pl.loop(0, F)
-    def _(k):
+    def forward(k, f2):
+        theirs = gated.at[at(k, rows, rows), at(f2, CS, CS)]
+        return remote(theirs, theirs, gf_ss.at[k * F + f2], gd_rs.at[k * F + f2], mate, c)
+
+    def gated_wait(k, f2):
+        theirs = gated.at[at(k, rows, rows), at(f2, CS, CS)]
+        remote(theirs, theirs, gd_ss.at[k * F + f2], gd_rs.at[k * F + f2], f2, c).wait_recv()
+
+    def pass_on(k):
+        for f2 in peers:
+            gated_wait(k, f2)
+            forward(k, f2).start()
+
+    half, mine_z = lax.rem(c, 2), c // 2
+
+    def ya_copy(k):
+        return remote(po.at[k, :, 1 - half], ya_in.at[k], ya_ss.at[k], ya_rs.at[k], f, c_mate)
+
+    def zb_copy(k, z):
+        return remote(pair.at[k, z], zb_in.at[k, mine_z], zb_ss.at[k * H + z], zb_rs.at[k * H + mine_z], f, 2 * z + half)
+
+    def fc_copy(k):
+        return remote(done.at[k], fc_in.at[f], fc_ss.at[k], fc_rs.at[f], k, c)
+
+    def gating(k):
         piece = at(k, rows, rows)
         pre = gate_own[piece]
         for j in range(1, F):
@@ -408,67 +420,42 @@
         for f2 in [mate] + peers:
             gated_copy(k, f2).start()
 
-    def forward(k, f2):
-        theirs = gated.at[at(k, rows, rows), at(f2, CS, CS)]
-        return remote(theirs, theirs, gf_ss.at[k * F + f2], gd_rs.at[k * F + f2], mate, c)
-
-    def gated_wait(k, f2):
-        theirs = gated.at[at(k, rows, rows), at(f2, CS, CS)]
-        remote(theirs, theirs, gd_ss.at[k * F + f2], gd_rs.at[k * F + f2], f2, c).wait_recv()
-
-    def pass_on(k):
-        for f2 in peers:
+    def partial_sums(k):
+        for f2 in [mate] + mates:
             gated_wait(k, f2)
-            forward(k, f2).start()
-
-    half, mine_z = lax.rem(c, 2), c // 2
-
-    def ya_copy(k):
-        return remote(po.at[k, :, 1 - half], ya_in.at[k], ya_ss.at[k], ya_rs.at[k], f, c_mate)
-
-    def zb_copy(k, z):
-        return remote(pair.at[k, z], zb_in.at[k, mine_z], zb_ss.at[k * H + z], zb_rs.at[k * H + mine_z], f, 2 * z + half)
-
-    def fc_copy(k):
-        return remote(done.at[k], fc_in.at[f], fc_ss.at[k], fc_rs.at[f], k, c)
-
-    pass_on(0)
-
-    @pl.loop(0, F + 2)
-    def _(k):
-        @pl.when(k + 1 < F)
-        def _():
-            pass_on(k + 1)
-
-        @pl.when(k < F)
-        def _():
-            gated_wait(k, mate)
-            for j in range(2, F, 2):
-                gated_wait(k, lax.rem(mate + j, F))
-            part = lax.dot_general(
-                gated[at(k, rows, rows)], out_w[...], (((1,), (1,)), ((), ())), preferred_element_type=f32
-            )
-            po[k] = part.astype(bf16).reshape(H, 2, R, DB)
-            ya_copy(k).start()
-
-        @pl.when((k >= 1) & (k < F + 1))
-        def _():
-            q = k - 1
-            ya_copy(q).wait_recv()
-            pair[q] = (po[q, :, half].astype(f32) + ya_in[q].astype(f32)).astype(bf16)
-            for j in range(1, H):
-                zb_copy(q, lax.rem(mine_z + j, H)).start()
-
-        @pl.when(k >= 2)
-        def _():
-            q = k - 2
-            total = pair[q, mine_z].astype(f32)
-            for j in range(1, H):
-                z = lax.rem(mine_z + j, H)
-                remote(pair.at[q, z], zb_in.at[q, z], zb_ss.at[q * H + z], zb_rs.at[q * H + z], f, 2 * z + half).wait_recv()
-                total = total + zb_in[q, z].astype(f32)
-            done[q] = total.astype(bf16)
-            pl.when(q != f)(lambda: fc_copy(q).start())
+        part = lax.dot_general(
+            gated[at(k, rows, rows)], out_w[...], (((1,), (1,)), ((), ())), preferred_element_type=f32
+        )
+        po[k] = part.astype(bf16).reshape(H, 2, R, DB)
+        ya_copy(k).start()
+
+    def pair_sums(k):
+        ya_copy(k).wait_recv()
+        pair[k] = (po[k, :, half].astype(f32) + ya_in[k].astype(f32)).astype(bf16)
+        for j in range(1, H):
+            zb_copy(k, lax.rem(mine_z + j, H)).start()
+
+    def whole_sums(k):
+        total = pair[k, mine_z].astype(f32)
+        for j in range(1, H):
+            z = lax.rem(mine_z + j, H)
+            remote(pair.at[k, z], zb_in.at[k, z], zb_ss.at[k * H + z], zb_rs.at[k * H + z], f, 2 * z + half).wait_recv()
+            total = total + zb_in[k, z].astype(f32)
+        done[k] = total.astype(bf16)
+        pl.when(k != f)(lambda: fc_copy(k).start())
+
+    def stages(k, h):
+        h = lax.cond(k < F, lambda: scan_block(k, h), lambda: h)
+        for lag, stage in enumerate((gating, pass_on, partial_sums, pair_sums, whole_sums)):
+            lag = LAGS[lag]
+
+            @pl.when((k >= lag) & (k < F + lag))
+            def _():
+                stage(k - lag)
+
+        return h
+
+    lax.fori_loop(0, F + LAGS[-1], stages, state[...])
 
     fc_in[f] = done[f]
     for f2 in range(F):

time: 83.8 us -> 76.9 us (0.918)
  Pallas kernels: 73.8 us -> 66.8 us
    pallas_call x1, Pallas kernels: 73.8 us -> 66.8 us  [shards(): pl.pallas_call(functools.partial(fused_kernel, F, G), out_shape=jax.Shape...]
where the time goes in v3:
time: 76.9 us; the launch traced here: 76.4 us
  Pallas kernels  66.8 us (87%)
  local copies, waits for them, and re-layouts  9.58 us (12%)
    pallas_call x1, Pallas kernels, shards(): pl.pallas_call(functools.partial(fused_kernel, F, G), out_shape=jax.Shape...  66.8 us
    unnamed x19, local copies, waits for them, and re-layouts  9.58 us

profile of v3, /device:TPU:0, one launch (start us, length us, event | category | flops | bytes accessed | tf_op | source)
XLA Modules:
  0.0 76.4 jit_solution(12065726913754516712)
XLA Ops:
  0.0 0.0 copy-start
  0.0 1.6 %copy-done = bf16[1024,1024]{1,0:T(8,128)(2,1)S(1)} copy-done((bf16[1024,1024]{1,0:T(8,128)(2,1)S(1)}, bf16[1024,1024]{1,0:T(8,128)(2,1)}, u32[]{:S(2)}) %copy-start) | copy-done | bytes 2097176
  1.6 0.0 copy-start.1
  1.6 1.2 %copy-done.1 = bf16[128,4096]{1,0:T(8,128)(2,1)S(1)} copy-done((bf16[128,4096]{1,0:T(8,128)(2,1)S(1)}, bf16[128,4096]{1,0:T(8,128)(2,1)}, u32[]{:S(2)}) %copy-start.1) | copy-done | bytes 1048600
  2.8 0.0 copy-start.2
  2.8 1.1 %copy-done.2 = bf16[1024,288]{0,1:T(8,128)(2,1)S(1)} copy-done((bf16[1024,288]{0,1:T(8,128)(2,1)S(1)}, bf16[1024,288]{0,1:T(8,128)(2,1)}, u32[]{:S(2)}) %copy-start.2) | copy-done | bytes 589848
  3.9 0.0 copy-start.3
  3.9 1.0 %copy-done.3 = bf16[256,1024]{1,0:T(8,128)(2,1)S(1)} copy-done((bf16[256,1024]{1,0:T(8,128)(2,1)S(1)}, bf16[256,1024]{1,0:T(8,128)(2,1)}, u32[]{:S(2)}) %copy-start.3) | copy-done | bytes 524312
  4.9 0.0 copy-start.4
  4.9 0.9 %copy-done.4 = bf16[128,1024]{1,0:T(8,128)(2,1)S(1)} copy-done((bf16[128,1024]{1,0:T(8,128)(2,1)S(1)}, bf16[128,1024]{1,0:T(8,128)(2,1)}, u32[]{:S(2)}) %copy-start.4) | copy-done | bytes 262168
  5.9 0.0 copy-start.5
  5.9 0.8 %copy-done.5 = f32[1024,16]{0,1:T(8,128)S(1)} copy-done((f32[1024,16]{0,1:T(8,128)S(1)}, f32[1024,16]{0,1:T(8,128)}, u32[]{:S(2)}) %copy-start.5) | copy-done | bytes 65560
  6.7 0.0 copy-start.6
  6.7 0.8 %copy-done.6 = f32[1024,16]{0,1:T(8,128)S(1)} copy-done((f32[1024,16]{0,1:T(8,128)S(1)}, f32[1024,16]{0,1:T(8,128)}, u32[]{:S(2)}) %copy-start.6) | copy-done | bytes 65560
  7.6 0.0 copy-start.7
  7.6 0.7 copy-done.7
  8.2 0.0 copy-start.8
  8.2 0.7 copy-done.8
  8.9 66.8 %shard_map.100 = bf16[16,4096]{1,0:T(8,128)(2,1)S(1)} custom-call(bf16[128,4096]{1,0:T(8,128)(2,1)S(1)} %copy-done.1, bf16[128,1024]{1,0:T(8,128)(2,1)S(1)} %copy-done.4, f32[16,1024]{1,0:T(8,128)S(1)} %bitcast.6, bf16[1024,1024]{1,0:T(8,128)(2,1)S(1)} %copy-done, bf16[288,1024]{1,0:T(8,128)(2,1)S(1)} %bitcast.5, bf16[256,1024]{1,0:T(8,128)(2,1)S(1)} %copy-done.3, ...), custom_call_target="tpu_custom_call" | custom-call | tf_op jit(solution)/shard_map/pallas_call | solution.py:541
  75.7 0.7 copy.12
Async XLA Ops:
  0.0 1.6 %copy-start = (bf16[1024,1024]{1,0:T(8,128)(2,1)S(1)}, bf16[1024,1024]{1,0:T(8,128)(2,1)}, u32[]{:S(2)}) copy-start(bf16[1024,1024]{1,0:T(8,128)(2,1)} %gate_h.1) | copy-start | bytes 6291460
  1.6 1.2 %copy-start.1 = (bf16[128,4096]{1,0:T(8,128)(2,1)S(1)}, bf16[128,4096]{1,0:T(8,128)(2,1)}, u32[]{:S(2)}) copy-start(bf16[128,4096]{1,0:T(8,128)(2,1)} %hidden.1) | copy-start | bytes 3145732
  2.8 1.1 %copy-start.2 = (bf16[1024,288]{0,1:T(8,128)(2,1)S(1)}, bf16[1024,288]{0,1:T(8,128)(2,1)}, u32[]{:S(2)}) copy-start(bf16[1024,288]{0,1:T(8,128)(2,1)} %param.14) | copy-start | bytes 1769476
  3.9 1.0 %copy-start.3 = (bf16[256,1024]{1,0:T(8,128)(2,1)S(1)}, bf16[256,1024]{1,0:T(8,128)(2,1)}, u32[]{:S(2)}) copy-start(bf16[256,1024]{1,0:T(8,128)(2,1)} %dt_h.1) | copy-start | bytes 1572868
  4.9 0.9 %copy-start.4 = (bf16[128,1024]{1,0:T(8,128)(2,1)S(1)}, bf16[128,1024]{1,0:T(8,128)(2,1)}, u32[]{:S(2)}) copy-start(bf16[128,1024]{1,0:T(8,128)(2,1)} %conv_h.1) | copy-start | bytes 786436
  5.9 0.8 %copy-start.5 = (f32[1024,16]{0,1:T(8,128)S(1)}, f32[1024,16]{0,1:T(8,128)}, u32[]{:S(2)}) copy-start(f32[1024,16]{0,1:T(8,128)} %param.12) | copy-start | bytes 196612
  6.7 0.8 %copy-start.6 = (f32[1024,16]{0,1:T(8,128)S(1)}, f32[1024,16]{0,1:T(8,128)}, u32[]{:S(2)}) copy-start(f32[1024,16]{0,1:T(8,128)} %param.17) | copy-start | bytes 196612
  7.6 0.7 copy-start.7
  8.2 0.7 copy-start.8

commit v4 on v3

--- a/solution.py
+++ b/solution.py
@@ -545,7 +545,7 @@
         out_specs=pl.BlockSpec(memory_space=pltpu.VMEM),
         scratch_shapes=scratch,
         compiler_params=pltpu.CompilerParams(
-            collective_id=0, has_side_effects=True, vmem_limit_bytes=48 * 2**20
+            collective_id=0, has_side_effects=True, vmem_limit_bytes=60 * 2**20
         ),
     )(
         hidden,

time: 76.9 us -> 70 us (0.910)
  local copies, waits for them, and re-layouts: 9.58 us -> 1.57 us
  Pallas kernels: 66.8 us -> 68.2 us
    unnamed x19 -> x1, local copies, waits for them, and re-layouts: 9.58 us -> 1.57 us
    pallas_call x1, Pallas kernels: 66.8 us -> 68.2 us  [shards(): pl.pallas_call(functools.partial(fused_kernel, F, G), out_shape=jax.Shape...]
where the time goes in v4:
time: 70 us; the launch traced here: 69.8 us
  Pallas kernels  68.2 us (97%)
  local copies, waits for them, and re-layouts  1.57 us (2%)
    pallas_call x1, Pallas kernels, shards(): pl.pallas_call(functools.partial(fused_kernel, F, G), out_shape=jax.Shape...  68.2 us
    unnamed x1, local copies, waits for them, and re-layouts  1.57 us

profile of v4, /device:TPU:0, one launch (start us, length us, event | category | flops | bytes accessed | tf_op | source)
XLA Modules:
  0.0 69.8 jit_solution(5012109187057155417)
XLA Ops:
  0.0 68.2 %shard_map.100 = bf16[16,4096]{1,0:T(8,128)(2,1)} custom-call(bf16[128,4096]{1,0:T(8,128)(2,1)} %hidden.1, bf16[128,1024]{1,0:T(8,128)(2,1)} %conv_h.1, f32[16,1024]{1,0:T(8,128)} %bitcast.6, bf16[1024,1024]{1,0:T(8,128)(2,1)} %gate_h.1, bf16[288,1024]{1,0:T(8,128)(2,1)} %bitcast.5, bf16[256,1024]{1,0:T(8,128)(2,1)} %dt_h.1, f32[1,1024]{1,0:T(1,128)} %bitcast.8, ...), custom_call_target="tpu_custom_call" | custom-call | tf_op jit(solution)/shard_map/pallas_call | solution.py:541
  68.3 1.6 %copy.12 = bf16[16,4096]{1,0:T(8,128)(2,1)} copy(bf16[16,4096]{1,0:T(8,128)(2,1)} %shard_map.100) | data formatting | bytes 262144
